TPU v7x, 1024 devices: a whole 8x8x8 slice. The times are simulated.
1024 devices in a mesh: section: 4 (over z_lo, core), rep: 4 (over z_hi), expert: 64 (over y, x).
Axes of the slice: x: 8, y: 8, z: 8 (z_hi: 4, z_lo: 2; z = z_hi * 2 + z_lo), core: 2. Of those that a mesh axis runs over, the one named last changes fastest.
Arguments:
- activations: bfloat16 [4, 4, 4096, 7168], P('section', 'rep', 'expert'), may hold values from -6 to 6
- routes: int32 [4, 4, 4096, 8], P('section', 'rep', 'expert'), may hold values from 0 to 255, all different within a row; in each aligned block of 64 rows (0 to 63, 64 to 127, ..., all dimensions but the last counted through in order) at most 2 rows name the same one
- gate_values: float32 [4, 4, 4096, 8], P('section', 'rep', 'expert'), may hold values from 0.1 to 1
- w_gate: bfloat16 [4, 7168, 8192], P('section', None, 'expert'), may hold values from -0.0625 to 0.0625
- w_up: bfloat16 [4, 7168, 8192], P('section', None, 'expert'), may hold values from -0.0625 to 0.0625
- w_down: bfloat16 [4, 8192, 7168], P('section', 'expert'), may hold values from -0.125 to 0.125
Outputs:
- handed: bfloat16 [4, 4, 4096, 7168], P('section', 'rep', 'expert')
- load_share: float32 [4, 4], P('section')
Inputs may be any that keep to these rules, and one draw needn't show every extreme that they name: The 8 routes of a token name different experts; in each aligned block of 64 tokens (the tokens of one device) at most 2 tokens name one expert.
All inputs are finite; a program needn't handle non-finite values.
Results may differ from a plain program's by a relative error of at most 0.012.
Values may be sent and summed in bfloat16 or wider, within the bound.
A program may use at most 32 MiB of HBM per device.

v0:
```python
import jax
import jax.numpy as jnp
from jax import lax
from jax.sharding import PartitionSpec as P

EXPERTS = 4
CAPACITY = 2


def from_behind(block, axis, distance):
    devices = range(lax.axis_size(axis))
    route = [((i - distance) % len(devices), i) for i in devices]
    return lax.ppermute(block, axis, route)


def route_tables(route_ids, gates):
    expert_ids = jnp.arange(EXPERTS, dtype=jnp.int32)
    matches = (route_ids[:, :, None] == expert_ids[None, None, :]).astype(jnp.float32)
    hits = jnp.sum(matches, axis=1)
    mass = jnp.sum(gates[:, :, None] * matches, axis=1)
    return (hits, mass)


def slot_picks(hits):
    before = jnp.cumsum(hits, axis=0) - hits
    slots = jnp.arange(CAPACITY).astype(jnp.float32)
    picks = hits[:, :, None] * (before[:, :, None] == slots[None, None, :]).astype(jnp.float32)
    return jnp.transpose(picks, (1, 2, 0))


def local(activations, routes, gate_values, w_gate, w_up, w_down):
    peers = lax.axis_size("expert")
    members = peers // EXPERTS
    highest = lax.Precision.HIGHEST
    rows_here = activations[0, 0]
    tok_here = rows_here.shape[0]
    width = rows_here.shape[1]
    hits, gate_mass = route_tables(routes[0, 0], gate_values[0, 0])
    slot_weights = gate_mass.astype(jnp.bfloat16)
    picks = slot_picks(hits)
    buffer = jnp.einsum(
        "ect,td->ecd", picks.astype(jnp.bfloat16), rows_here, preferred_element_type=jnp.float32
    ).astype(jnp.bfloat16)
    buffer_weights = jnp.einsum(
        "ect,te->ec", picks, slot_weights.astype(jnp.float32), precision=highest
    )
    copies = jnp.repeat(buffer, members, axis=0)
    copy_weights = jnp.repeat(buffer_weights, members, axis=0).astype(jnp.bfloat16)
    gate_w = w_gate[0]
    up_w = w_up[0]
    down_w = w_down[0]
    got_rows, got_weights = (
        lax.all_to_all(copies, "expert", split_axis=0, concat_axis=0, tiled=True),
        lax.all_to_all(copy_weights, "expert", split_axis=0, concat_axis=0, tiled=True),
    )
    sources = got_rows.shape[0]
    slots = got_rows.shape[1]
    flat = got_rows.reshape(sources * slots, width)
    gate_proj = jnp.dot(flat, gate_w, preferred_element_type=jnp.float32)
    up_proj = jnp.dot(flat, up_w, preferred_element_type=jnp.float32)
    hidden = (jax.nn.silu(gate_proj) * up_proj).astype(jnp.bfloat16)
    partial_out = jnp.dot(hidden, down_w, preferred_element_type=jnp.float32)
    scale = got_weights.reshape(sources * slots).astype(jnp.float32)
    weighted = (scale[:, None] * partial_out).astype(jnp.bfloat16)
    weighted = weighted.reshape(sources, slots, width)
    returned = lax.all_to_all(weighted, "expert", split_axis=0, concat_axis=0, tiled=True)
    per_expert = jnp.sum(
        returned.astype(jnp.float32).reshape(EXPERTS, members, CAPACITY, width), axis=1
    )
    mixed = jnp.einsum("ect,ecd->td", picks, per_expert, precision=highest).astype(jnp.bfloat16)
    handed = from_behind(mixed, "section", 1)
    total_load = lax.psum(jnp.sum(gate_mass, axis=0), ("rep", "expert"))
    load_share = total_load / jnp.float32(lax.axis_size("rep") * peers * tok_here)
    return (handed[None, None], load_share[None])


def solution(mesh):
    placed = (
        P("section", "rep", "expert", None),
        P("section", "rep", "expert", None),
        P("section", "rep", "expert", None),
        P("section", None, "expert"),
        P("section", None, "expert"),
        P("section", "expert", None),
    )
    return jax.shard_map(
        local,
        mesh=mesh,
        in_specs=placed,
        out_specs=(P("section", "rep", "expert", None), P("section", None)),
        check_vma=False,
    )
```

profile of v0, /device:TPU:128, one launch (start us, length us, event | category | flops | bytes accessed | tf_op | source)
XLA Modules:
  0.0 914.3 jit_solution(11878464313953279001)
XLA Ops:
  0.6 0.0 copy-start
  0.7 1.0 select_reduce_fusion
  1.6 0.1 copy.27
  1.7 0.1 copy.30
  1.8 0.1 reduce_window_sum.13
  1.9 0.1 copy.29
  2.0 0.1 compare_select_fusion
  2.0 0.1 fusion.23
  2.2 0.1 copy.36
  2.3 0.1 broadcast_in_dim.8
  2.4 0.1 convert_element_type.59
  2.5 0.7 copy.31
  3.2 13.5 %all-to-all-start = ((bf16[64,1,2]{2,1,0:T(2,128)(2,1)}), bf16[64,1,2]{2,1,0:T(2,128)(2,1)S(1)}, u32[]{:S(2)}, u32[]{:S(2)}) async-start(bf16[64,1,2]{2,1,0:T(2,128)(2,1)} %copy.31), calls=%async_computation | async-start | bytes 65536 | tf_op jit(solution)/shard_map/all_to_all | solution.py:54
  16.7 1.5 convolution_convert_fusion
  18.2 0.1 copy.32
  18.3 10.3 %all-to-all-done = bf16[64,1,2]{2,1,0:T(2,128)(2,1)S(1)} async-done(((bf16[64,1,2]{2,1,0:T(2,128)(2,1)}), bf16[64,1,2]{2,1,0:T(2,128)(2,1)S(1)}, u32[]{:S(2)}, u32[]{:S(2)}) %all-to-all-start) | async-done | bytes 288 | tf_op jit(solution)/shard_map/all_to_all | solution.py:54
  28.6 2.2 broadcast_in_dim.18
  30.8 5.5 all-to-all-start.1
  36.3 0.1 convert_reduce_fusion.1
  36.4 0.1 reshape.63
  36.5 45.6 %all-to-all-done.1 = bf16[64,2,7168]{2,1,0:T(2,128)(2,1)} async-done(((bf16[64,2,7168]{2,1,0:T(2,128)(2,1)}), bf16[64,2,7168]{2,1,0:T(2,128)(2,1)}, u32[]{:S(2)}, u32[]{:S(2)}) %all-to-all-start.1) | async-done | bytes 1835040 | tf_op jit(solution)/shard_map/all_to_all | solution.py:53
  82.1 4.9 reshape.59
  87.1 2.7 fusion.5
  89.7 4.5 fusion
  94.3 4.7 reshape.60
  99.0 51.8 %all_to_all.16 = bf16[64,2,7168]{2,1,0:T(2,128)(2,1)S(1)} all-to-all(bf16[64,2,7168]{2,1,0:T(2,128)(2,1)} %reshape.60), channel_id=1, replica_groups=mesh['section'=4,'rep'=4,'expert'=64] {'expert'}, dimensions={0} | all-to-all | bytes 3670016 | tf_op jit(solution)/shard_map/all_to_all | solution.py:66
  150.8 1.5 convert_reduce_fusion
  152.4 2.7 fusion.1
  155.0 1.9 collective-permute-start
  156.9 755.9 %psum.7 = f32[4]{0:T(128)S(1)} all-reduce(f32[4]{0:T(128)S(1)} %get-tuple-element.2), channel_id=1, replica_groups=mesh['section'=4,'rep'=4,'expert'=64] {'rep','expert'}, use_global_device_ids=true, to_apply=%region_5.6 | all-reduce | flops 4 | bytes 32 | tf_op jit(solution)/shard_map/psum | solution.py:72
  912.8 0.5 multiply_bitcast_fusion
  913.4 0.9 copy.44
  (4 shorter events, 0.0 us)
Async XLA Ops:
  0.6 89.1 %copy-start = (bf16[1,128,7168]{2,1,0:T(8,128)(2,1)S(1)}, bf16[1,128,7168]{2,1,0:T(8,128)(2,1)}, u32[]{:S(2)}) copy-start(bf16[1,128,7168]{2,1,0:T(8,128)(2,1)} %param.11) | copy-start | bytes 5505028
  3.2 25.4 %all-to-all-start = ((bf16[64,1,2]{2,1,0:T(2,128)(2,1)}), bf16[64,1,2]{2,1,0:T(2,128)(2,1)S(1)}, u32[]{:S(2)}, u32[]{:S(2)}) async-start(bf16[64,1,2]{2,1,0:T(2,128)(2,1)} %copy.31), calls=%async_computation | async-start | bytes 65536 | tf_op jit(solution)/shard_map/all_to_all | solution.py:54
  30.8 51.4 %all-to-all-start.1 = ((bf16[64,2,7168]{2,1,0:T(2,128)(2,1)}), bf16[64,2,7168]{2,1,0:T(2,128)(2,1)}, u32[]{:S(2)}, u32[]{:S(2)}) async-start(bf16[64,2,7168]{2,1,0:T(2,128)(2,1)} %bitcast.47), calls=%async_computation.1 | async-start | bytes 3670016 | tf_op jit(solution)/shard_map/all_to_all | solution.py:53
  155.0 758.3 %collective-permute-start = (bf16[64,7168]{1,0:T(8,128)(2,1)}, bf16[64,7168]{1,0:T(8,128)(2,1)S(1)}, u32[]{:S(2)}, u32[]{:S(2)}) collective-permute-start(bf16[64,7168]{1,0:T(8,128)(2,1)} %fusion.1), channel_id=1, source_target_pairs={{768,0},{0,256},{256,512},{512,768},{769,1},{1,257},{257,513},{513... | collective-permute-start | bytes 2752520 | tf_op jit(solution)/shard_map/ppermute | solution.py:13
where the time goes:
time: 915 us; the launch traced here: 914 us
  blocking collectives  808 us (88%)
  waiting for transfers between devices  55.9 us (6%)
  starting transfers between devices  20.9 us (2%)
  local copies, waits for them, and re-layouts  14.2 us (2%)
  matrix products  11.5 us (1%)
    psum x1, blocking collectives, local(): total_load = lax.psum(jnp.sum(gate_mass, axis=0), ('rep', 'expert'))  756 us
    all_to_all x1, blocking collectives, local(): lax.all_to_all(weighted, 'expert', split_axis=0, concat_axis=0, tiled=True)  51.8 us
    all_to_all x1, waiting for transfers between devices, local(): lax.all_to_all(copies, 'expert', split_axis=0, concat_axis=0, tiled=True)  45.6 us
  transfers between devices with their start and end apart: 3, of which 2 were waited for; matrix products, arithmetic and copies ran while one was open for 0% of the time, Pallas kernels for 0%

commit v1 on v0

v1 whole, which is shorter than its diff:
```python
import functools

import jax
import jax.numpy as jnp
from jax import lax
from jax.experimental import pallas as pl
from jax.experimental.pallas import tpu as pltpu
from jax.sharding import PartitionSpec as P

MESH = pl.DeviceIdType.MESH
BF16 = jnp.bfloat16
F32 = jnp.float32
EXPERTS = 4
N = 8
HALF = N // 2
UNIT = 1024
LANES = 128


def iota(shape, axis):
    return lax.broadcasted_iota(jnp.int32, shape, axis)


def dot(a, b):
    return jnp.dot(a, b, preferred_element_type=F32)


def one_hot(mask):
    return jnp.where(mask, 1.0, 0.0).astype(BF16)


def routing(routes_ref, gates_ref):
    tokens = routes_ref.shape[1]
    rows = EXPERTS * 2 * 8
    row = iota((rows, tokens), 0)
    expert = lax.div(row, 16)
    slot = lax.rem(lax.div(row, 8), 2).astype(F32)
    hits = jnp.zeros((rows, tokens), F32)
    mass = jnp.zeros((rows, tokens), F32)
    for k in range(routes_ref.shape[0]):
        same = routes_ref[k : k + 1, :] == expert
        hits = hits + jnp.where(same, 1.0, 0.0)
        mass = mass + jnp.where(same, gates_ref[k : k + 1, :], 0.0)
    earlier = one_hot(iota((tokens, tokens), 0) < iota((tokens, tokens), 1))
    before = dot(hits.astype(BF16), earlier)
    picks = jnp.where(before == slot, hits, 0.0)
    return picks, mass


def expert_mass(routes_ref, gates_ref):
    tokens = routes_ref.shape[1]
    expert = iota((8, tokens), 0)
    mass = jnp.zeros((8, tokens), F32)
    for k in range(routes_ref.shape[0]):
        same = routes_ref[k : k + 1, :] == expert
        mass = mass + jnp.where(same, gates_ref[k : k + 1, :], 0.0)
    return jnp.broadcast_to(jnp.sum(mass, axis=1, keepdims=True), (8, LANES))


def layer_kernel(
    sizes,
    routes_ref, gates_ref, acts_hbm, gate_hbm, up_hbm, down_hbm,
    own_ref, both_ref, pw_ref, load_ref,
    acts, w_in, w_out, picked, first_own, first_both, rows, pw_out,
    mass_out, mass_y, mass_x, mass_z,
    part, rung, send_own, send_both, got_own, got_both, last_own, last_both,
    load_sem, pw_sem, my_sem, mx_sem, mz_sem, fo_sem, fb_sem,
    go_sem, gb_sem, gr_sem, rr_sem, so_sem, sb_sem, lo_sem, lb_sem,
):
    sections, reps, own_units, both_units = sizes
    own_w, both_w = own_units * UNIT, both_units * UNIT
    tokens = acts.shape[0]
    section, rep, index = (lax.axis_index(a) for a in ("section", "rep", "expert"))
    x, y = lax.rem(index, N), lax.div(index, N)
    expert, side = lax.div(y, 2), lax.rem(y, 2)

    def at(x_, y_):
        return {"expert": lax.rem(y_ + N, N) * N + lax.rem(x_ + N, N)}

    def block(d):
        return lax.rem(x + d + N, N)

    def remote(src, dst, sems, i, device):
        return pltpu.make_async_remote_copy(
            src_ref=src, dst_ref=dst, send_sem=sems.at[(0, *i)], recv_sem=sems.at[(1, *i)],
            device_id=device, device_id_type=MESH,
        )

    sent = []

    def start(copy):
        copy.start()
        sent.append(copy)
        return copy

    loads = [
        pltpu.make_async_copy(acts_hbm, acts, load_sem.at[0]),
        pltpu.make_async_copy(gate_hbm, w_in.at[:, 0:LANES], load_sem.at[1]),
        pltpu.make_async_copy(up_hbm, w_in.at[:, LANES : 2 * LANES], load_sem.at[2]),
        pltpu.make_async_copy(down_hbm, w_out, load_sem.at[3]),
    ]
    for load in loads:
        load.start()

    ahead = {"section": lax.rem(section + 1, sections)}
    behind = {"section": lax.rem(section + sections - 1, sections)}
    barrier = pltpu.get_barrier_semaphore()
    for d in range(1, N):
        for device in (at(x, y + d - N), at(x + d - N, y)):
            pl.semaphore_signal(barrier, inc=1, device_id=device, device_id_type=MESH)
    for d in range(1, reps):
        pl.semaphore_signal(barrier, inc=1, device_id={"rep": lax.rem(rep + d, reps)}, device_id_type=MESH)
    for d in range(N):
        pl.semaphore_signal(barrier, inc=1, device_id={**behind, **at(x, y + d - N)}, device_id_type=MESH)

    picks, mass = routing(routes_ref, gates_ref)
    pw_out[...] = jnp.where(picks > 0, mass, 0.0).astype(BF16)
    mass_out[0] = expert_mass(routes_ref, gates_ref)
    spread = one_hot(iota((tokens, 8 * tokens), 0) == lax.rem(iota((tokens, 8 * tokens), 1), tokens))
    wide = dot(picks.astype(BF16), spread)
    wide_rows, wide_cols = iota(wide.shape, 0), iota(wide.shape, 1)
    wide = jnp.where(lax.rem(wide_rows, 8) == lax.div(wide_cols, tokens), wide, 0.0).astype(BF16)
    loads[0].wait()

    def pick_unit(u):
        stacked = jnp.concatenate(
            [acts[:, u * UNIT + i * LANES : u * UNIT + (i + 1) * LANES] for i in range(8)], axis=0
        )
        picked[:, u] = dot(wide, stacked).astype(BF16).reshape(EXPERTS, 16, LANES)

    for u in (*range(own_units), *range(own_units + both_units, 2 * own_units + both_units)):
        pick_unit(u)
    pl.semaphore_wait(barrier, (N - 1) * 2 + (reps - 1) + N)

    own_copies, both_copies, mass_copies = [], [], []
    for d in range(1, N):
        to_y = lax.rem(y + d, N)
        own_copies.append(start(remote(
            picked.at[lax.div(to_y, 2), pl.ds(lax.rem(to_y, 2) * (own_units + both_units), own_units)],
            first_own.at[y], fo_sem, (d,), at(x, to_y),
        )))
    first_own[y] = picked[expert, pl.ds(side * (own_units + both_units), own_units)]
    for u in range(own_units, own_units + both_units):
        pick_unit(u)
    for d in range(1, N):
        to_y = lax.rem(y + d, N)
        both_copies.append(start(remote(
            picked.at[lax.div(to_y, 2), pl.ds(own_units, both_units)],
            first_both.at[y], fb_sem, (d,), at(x, to_y),
        )))
    first_both[y] = picked[expert, pl.ds(own_units, both_units)]
    pw_copy = start(remote(pw_out, pw_ref, pw_sem, (), {**ahead}))
    for d in range(1, N):
        mass_copies.append(start(remote(mass_out.at[0], mass_y.at[y], my_sem, (d,), at(x, y + d - N))))
    mass_y[y] = mass_out[0]

    perm_rows, perm_cols = iota((128, 128), 0), iota((128, 128), 1)

    def inner(k):
        return lax.rem(lax.div(k, 2), 8) * 16 + lax.rem(k, 2) * 8 + lax.div(k, 16)

    gather_perm = one_hot(perm_cols == inner(perm_rows))
    scatter_perm = one_hot(perm_rows == inner(perm_cols))

    def assemble(buf, k):
        mixed = dot(gather_perm, buf[:, k].reshape(128, LANES)).astype(BF16)
        return jnp.concatenate([mixed[i * 16 : (i + 1) * 16] for i in range(8)], axis=1)

    def own_cols(first=0, width=own_w, mine=True):
        which = side if mine else 1 - side
        return pl.ds(pl.multiple_of(which * (own_w + both_w) + first, LANES), width)

    def both_cols(first=0, width=both_w):
        return pl.ds(own_w + first, width)

    def gather_copy(is_own, way, hop):
        sign = 1 if way == 0 else -1
        width = own_w if is_own else both_w
        first = 0
        if hop == HALF:
            width //= 2
            first = way * width
        cols = own_cols(first, width) if is_own else both_cols(first, width)
        piece = rows.at[block(-sign * (hop - 1)), :, cols]
        return remote(piece, piece, go_sem if is_own else gb_sem, (way, hop - 1), at(x + sign, y))

    def rung_copy(i, d, first=0, width=own_w):
        piece = rows.at[block(d), :, own_cols(first, width)]
        return remote(piece, piece, gr_sem, (i,), at(x, y + 1 - 2 * side))

    gathers = {}
    rungs = []
    for copy in own_copies:
        copy.wait_recv()
    for k in range(own_units):
        rows[x, :, own_cols(k * UNIT, UNIT)] = assemble(first_own, k)
    for way in range(2):
        gathers[True, way, 1] = start(gather_copy(True, way, 1))
    rungs.append(start(rung_copy(0, 0)))
    for copy in both_copies:
        copy.wait_recv()
    for k in range(both_units):
        rows[x, :, both_cols(k * UNIT, UNIT)] = assemble(first_both, k)
    for way in range(2):
        gathers[False, way, 1] = start(gather_copy(False, way, 1))

    for copy in mass_copies:
        copy.wait_recv()
    mass_out[1] = functools.reduce(jnp.add, [mass_y[i] for i in range(N)])
    mass_x[x] = mass_out[1]
    mass_copies = [
        start(remote(mass_out.at[1], mass_x.at[x], mx_sem, (d,), at(x + d - N, y))) for d in range(1, N)
    ]

    for hop in range(1, HALF):
        for is_own in (True, False):
            for way in range(2):
                gathers[is_own, way, hop].wait_recv()
                gathers[is_own, way, hop + 1] = start(gather_copy(is_own, way, hop + 1))
                if is_own:
                    rungs.append(start(rung_copy(len(rungs), (-1 if way == 0 else 1) * hop)))
        if hop == 1:
            for copy in mass_copies:
                copy.wait_recv()
            mass_out[2] = functools.reduce(jnp.add, [mass_x[i] for i in range(N)])
            mass_z[rep] = mass_out[2]
            mass_copies = [
                start(remote(mass_out.at[2], mass_z.at[rep], mz_sem, (d,), {"rep": lax.rem(rep + d, reps)}))
                for d in range(1, reps)
            ]
    for way in range(2):
        gathers[True, way, HALF].wait_recv()
        width = own_w // 2
        rungs.append(start(rung_copy(len(rungs), HALF, way * width, width)))

    step = 512

    def project(total, first, width):
        def body(j, total):
            cols = pl.ds(pl.multiple_of(first + j * step, step), step)
            return total + dot(rows[:, :, cols].reshape(128, step), w_in[cols, :])

        return lax.fori_loop(0, width // step, body, total)

    loads[1].wait()
    loads[2].wait()
    total = project(jnp.zeros((128, 2 * LANES), F32), side * (own_w + both_w), own_w)
    for way in range(2):
        gathers[False, way, HALF].wait_recv()
    total = project(total, own_w, both_w)
    for copy in rungs:
        copy.wait_recv()
    total = project(total, (1 - side) * (own_w + both_w), own_w)
    gate, up = total[:, :LANES], total[:, LANES:]
    hidden = (gate / (1.0 + jnp.exp(-gate)) * up).astype(BF16)
    loads[3].wait()

    def down(first, width):
        def body(j, carry):
            cols = pl.ds(pl.multiple_of(first + j * step, step), step)
            part[:, :, cols] = dot(hidden, w_out[:, cols]).astype(BF16).reshape(N, 16, step)
            return carry

        lax.fori_loop(0, width // step, body, 0)

    order = [HALF]
    for d in range(HALF - 1, 0, -1):
        order += [d, -d]
    order.append(0)
    down((1 - side) * (own_w + both_w), own_w)
    over = {}
    for i, d in enumerate(order):
        over[d] = start(remote(
            part.at[block(d), :, own_cols(mine=False)], rung.at[block(d)], rr_sem, (i,), at(x, y + 1 - 2 * side),
        ))

    def scatter_copy(is_own, way, hop, src):
        dst = (got_own if is_own else got_both).at[way, hop - 1]
        if hop == 1:
            dst = dst.at[:, 0 : (own_w if is_own else both_w) // 2]
        return remote(src, dst, so_sem if is_own else sb_sem, (way, hop - 1), at(x + 1 - 2 * way, y))

    scatters = {}
    down(own_w, both_w)
    for way in range(2):
        src = part.at[block(HALF), :, both_cols(way * (both_w // 2), both_w // 2)]
        scatters[False, way, 1] = start(scatter_copy(False, way, 1, src))
    down(side * (own_w + both_w), own_w)

    def mine(is_own, d):
        if is_own:
            return part[block(d), :, own_cols()].astype(F32) + rung[block(d)].astype(F32)
        return part[block(d), :, both_cols()].astype(F32)

    over[HALF].wait_recv()
    send_own[0, 0] = mine(True, HALF).astype(BF16)
    for way in range(2):
        src = send_own.at[0, 0, :, way * (own_w // 2) : (way + 1) * (own_w // 2)]
        scatters[True, way, 1] = start(scatter_copy(True, way, 1, src))
    for hop in range(2, HALF + 1):
        for is_own in (False, True):
            send, got = (send_own, got_own) if is_own else (send_both, got_both)
            width = own_w if is_own else both_w
            for way in range(2):
                d = (1 - 2 * way) * (HALF + 1 - hop)
                if is_own:
                    over[d].wait_recv()
                scatters[is_own, way, hop - 1].wait_recv()
                value = mine(is_own, d)
                if hop == 2:
                    left, right = way * (width // 2), (way + 1) * (width // 2)
                    came = got[way, 0, :, 0 : width // 2].astype(F32)
                    halves = [value[:, : width // 2], value[:, width // 2 :]]
                    halves[way] = halves[way] + came
                    value = jnp.concatenate(halves, axis=1)
                else:
                    value = value + got[way, hop - 2].astype(F32)
                send[way, hop - 1] = value.astype(BF16)
                scatters[is_own, way, hop] = start(scatter_copy(is_own, way, hop, send.at[way, hop - 1]))

    last_copies = []
    for is_own in (False, True):
        got, last, landing, sems = (
            (got_own, last_own, own_ref, lo_sem) if is_own else (got_both, last_both, both_ref, lb_sem)
        )
        if is_own:
            over[0].wait_recv()
        for way in range(2):
            scatters[is_own, way, HALF].wait_recv()
        value = mine(is_own, 0)
        for way in range(2):
            value = value + got[way, HALF - 1].astype(F32)
        value = value.astype(BF16)
        for k in range(own_units if is_own else both_units):
            stacked = jnp.concatenate(
                [value[:, k * UNIT + i * LANES : k * UNIT + (i + 1) * LANES] for i in range(8)], axis=0
            )
            last[:, k] = dot(scatter_perm, stacked).astype(BF16).reshape(N, 16, LANES)
        for d in range(N):
            to_y = lax.rem(y + d, N)
            last_copies.append(start(remote(
                last.at[to_y], landing.at[expert, side], sems, (d,), {**ahead, **at(x, to_y)},
            )))

    for copy in mass_copies:
        copy.wait_recv()
    load_ref[...] = functools.reduce(jnp.add, [mass_z[i] for i in range(reps)])
    pw_copy.wait_recv()
    for copy in last_copies:
        copy.wait_recv()
    for copy in sent:
        copy.wait_send()


def spread_kernel(own_units, both_units, count, own_ref, both_ref, pw_ref, load_ref, out_ref, share_ref):
    tokens = pw_ref.shape[1]
    spread = one_hot(iota((8 * tokens, tokens), 1) == lax.rem(iota((8 * tokens, tokens), 0), tokens))
    wide = lax.dot_general(spread, pw_ref[...], (((1,), (1,)), ((), ())), preferred_element_type=F32)
    wide_rows, wide_cols = iota(wide.shape, 0), iota(wide.shape, 1)
    wide = jnp.where(lax.rem(wide_cols, 8) == lax.div(wide_rows, tokens), wide, 0.0).astype(BF16)
    for u in range(2 * own_units + both_units):
        if u < own_units:
            value = own_ref[:, 0, u].astype(F32)
        elif u < own_units + both_units:
            value = both_ref[:, 0, u - own_units].astype(F32) + both_ref[:, 1, u - own_units].astype(F32)
        else:
            value = own_ref[:, 1, u - own_units - both_units].astype(F32)
        value = value.reshape(EXPERTS * 16, LANES)
        high = value.astype(BF16)
        low = (value - high.astype(F32)).astype(BF16)
        both = dot(wide, jnp.concatenate([high, low], axis=1))
        both = (both[:, :LANES] + both[:, LANES:]).astype(BF16)
        for i in range(8):
            out_ref[:, u * UNIT + i * LANES : u * UNIT + (i + 1) * LANES] = both[i * tokens : (i + 1) * tokens]
    lane, row = iota((8, LANES), 1), iota((8, LANES), 0)
    picked = jnp.sum(jnp.where(lane == row, load_ref[...], 0.0), axis=0, keepdims=True)
    share_ref[...] = picked[:, :EXPERTS] / count


def local(activations, routes, gate_values, w_gate, w_up, w_down):
    acts = activations[0, 0]
    tokens, width = acts.shape
    sections, reps = lax.axis_size("section"), lax.axis_size("rep")
    own_units = width // UNIT * 2 // 7
    both_units = width // UNIT - 2 * own_units
    own_w, both_w = own_units * UNIT, both_units * UNIT
    vmem = pl.BlockSpec(memory_space=pltpu.VMEM)
    hbm = pl.BlockSpec(memory_space=pl.ANY)
    dma = pltpu.SemaphoreType.DMA
    outs = pl.pallas_call(
        functools.partial(layer_kernel, (sections, reps, own_units, both_units)),
        out_shape=(
            jax.ShapeDtypeStruct((EXPERTS, 2, own_units, 16, LANES), BF16),
            jax.ShapeDtypeStruct((EXPERTS, 2, both_units, 16, LANES), BF16),
            jax.ShapeDtypeStruct((EXPERTS * 16, tokens), BF16),
            jax.ShapeDtypeStruct((8, LANES), F32),
        ),
        in_specs=[vmem, vmem, hbm, hbm, hbm, hbm],
        out_specs=(vmem, vmem, vmem, vmem),
        scratch_shapes=[
            pltpu.VMEM((tokens, width), BF16),
            pltpu.VMEM((width, 2 * LANES), BF16),
            pltpu.VMEM((LANES, width), BF16),
            pltpu.VMEM((EXPERTS, 2 * own_units + both_units, 16, LANES), BF16),
            pltpu.VMEM((N, own_units, 16, LANES), BF16),
            pltpu.VMEM((N, both_units, 16, LANES), BF16),
            pltpu.VMEM((N, 16, width), BF16),
            pltpu.VMEM((EXPERTS * 16, tokens), BF16),
            pltpu.VMEM((3, 8, LANES), F32),
            pltpu.VMEM((N, 8, LANES), F32),
            pltpu.VMEM((N, 8, LANES), F32),
            pltpu.VMEM((reps, 8, LANES), F32),
            pltpu.VMEM((N, 16, width), BF16),
            pltpu.VMEM((N, 16, own_w), BF16),
            pltpu.VMEM((2, HALF, 16, own_w), BF16),
            pltpu.VMEM((2, HALF, 16, both_w), BF16),
            pltpu.VMEM((2, HALF, 16, own_w), BF16),
            pltpu.VMEM((2, HALF, 16, both_w), BF16),
            pltpu.VMEM((N, own_units, 16, LANES), BF16),
            pltpu.VMEM((N, both_units, 16, LANES), BF16),
            dma((4,)),
            dma((2,)),
            dma((2, N)),
            dma((2, N)),
            dma((2, reps)),
            dma((2, N)),
            dma((2, N)),
            dma((2, 2, HALF)),
            dma((2, 2, HALF)),
            dma((2, N + 1)),
            dma((2, N)),
            dma((2, 2, HALF)),
            dma((2, 2, HALF)),
            dma((2, N)),
            dma((2, N)),
        ],
        compiler_params=pltpu.CompilerParams(
            collective_id=0, has_side_effects=True, vmem_limit_bytes=48 * 2**20
        ),
        name="layer",
    )(routes[0, 0].T, gate_values[0, 0].T, acts, w_gate[0], w_up[0], w_down[0])
    count = float(reps * lax.axis_size("expert") * tokens)
    handed, share = pl.pallas_call(
        functools.partial(spread_kernel, own_units, both_units, count),
        out_shape=(
            jax.ShapeDtypeStruct((tokens, width), BF16),
            jax.ShapeDtypeStruct((1, EXPERTS), F32),
        ),
        in_specs=[vmem] * 4,
        out_specs=(vmem, vmem),
        name="spread",
    )(*outs)
    return handed[None, None], share


def solution(mesh):
    placed = (
        P("section", "rep", "expert", None),
        P("section", "rep", "expert", None),
        P("section", "rep", "expert", None),
        P("section", None, "expert"),
        P("section", None, "expert"),
        P("section", "expert", None),
    )
    return jax.shard_map(
        local,
        mesh=mesh,
        in_specs=placed,
        out_specs=(P("section", "rep", "expert", None), P("section", None)),
        check_vma=False,
    )
```

time: 915 us -> 84.5 us (0.09)
  the two profiles are of different devices: /device:TPU:128 before, /device:TPU:1 now
where the time goes in v1:
time: 84.5 us; the launch traced here: 84.2 us
  Pallas kernels  75.6 us (89%)
  local copies, waits for them, and re-layouts  7.98 us (9%)
    pallas_call x1, Pallas kernels, local(): pl.pallas_call(functools.partial(layer_kernel, (sections, reps, own_units...  72.9 us
    unnamed x18, local copies, waits for them, and re-layouts  7.98 us
    pallas_call x1, Pallas kernels, local(): pl.pallas_call(functools.partial(spread_kernel, own_units, both_units, co...  2.62 us

profile of v1, /device:TPU:1, one launch (start us, length us, event | category | flops | bytes accessed | tf_op | source)
XLA Modules:
  0.0 84.2 jit_solution(10816734574075312828)
XLA Ops:
  0.6 0.0 copy-start
  0.6 1.5 %copy-done = bf16[1,7168,128]{2,1,0:T(8,128)(2,1)S(1)} copy-done((bf16[1,7168,128]{2,1,0:T(8,128)(2,1)S(1)}, bf16[1,7168,128]{2,1,0:T(8,128)(2,1)}, u32[]{:S(2)}) %copy-start) | copy-done | bytes 1835032
  2.1 0.0 copy-start.1
  2.1 1.5 %copy-done.1 = bf16[1,7168,128]{2,1,0:T(8,128)(2,1)S(1)} copy-done((bf16[1,7168,128]{2,1,0:T(8,128)(2,1)S(1)}, bf16[1,7168,128]{2,1,0:T(8,128)(2,1)}, u32[]{:S(2)}) %copy-start.1) | copy-done | bytes 1835032
  3.6 0.0 copy-start.2
  3.6 1.2 %copy-done.2 = bf16[1,1,64,7168]{3,2,1,0:T(8,128)(2,1)S(1)} copy-done((bf16[1,1,64,7168]{3,2,1,0:T(8,128)(2,1)S(1)}, bf16[1,1,64,7168]{3,2,1,0:T(8,128)(2,1)}, u32[]{:S(2)}) %copy-start.2) | copy-done | bytes 917528
  4.8 0.0 copy-start.6
  4.8 0.7 copy-done.6
  5.5 0.0 copy-start.7
  5.5 0.7 copy-done.7
  6.2 72.9 %layer.1 = (bf16[4,2,2,16,128]{4,3,2,1,0:T(8,128)(2,1)S(1)}, bf16[4,2,3,16,128]{4,3,2,1,0:T(8,128)(2,1)S(1)}, bf16[64,64]{1,0:T(8,128)(2,1)S(1)}, f32[8,128]{1,0:T(8,128)S(1)}) custom-call(s32[8,64]{1,0:T(8,128)S(1)} %bitcast.14, f32[8,64]{1,0:T(8,128)S(1)} %bitcast.15, bf16[64,7168]{1,0:T(8,128)(2,1)S(1)} %bitcast.13, bf16[7168,128]{1,0:T(8,128)(2,1)S(1)} %bitcast.11, ...), custom_call_target="tpu_custom_call" | custom-call | tf_op jit(solution)/shard_map/layer/pallas_call | solution.py:390
  79.1 0.0 copy-start.3
  79.1 0.6 copy-done.3
  79.8 0.0 copy-start.4
  79.8 0.6 copy-done.4
  80.4 0.0 copy-start.5
  80.4 0.6 copy-done.5
  81.0 0.0 copy-start.8
  81.0 0.6 copy-done.8
  81.6 2.6 %spread.1 = (bf16[64,7168]{1,0:T(8,128)(2,1)}, f32[1,4]{1,0:T(1,128)}) custom-call(bf16[4,2,2,16,128]{4,3,2,1,0:T(8,128)(2,1)} %copy-done.4, bf16[4,2,3,16,128]{4,3,2,1,0:T(8,128)(2,1)} %copy-done.3, bf16[64,64]{1,0:T(8,128)(2,1)} %copy-done.5, f32[8,128]{1,0:T(8,128)} %copy-done.8), custom_call_target="tpu_custom_call" | custom-call | tf_op jit(solution)/shard_map/spread/pallas_call | solution.py:443
Async XLA Ops:
  0.6 1.5 %copy-start = (bf16[1,7168,128]{2,1,0:T(8,128)(2,1)S(1)}, bf16[1,7168,128]{2,1,0:T(8,128)(2,1)}, u32[]{:S(2)}) copy-start(bf16[1,7168,128]{2,1,0:T(8,128)(2,1)} %param.9) | copy-start | bytes 5505028
  2.1 1.5 %copy-start.1 = (bf16[1,7168,128]{2,1,0:T(8,128)(2,1)S(1)}, bf16[1,7168,128]{2,1,0:T(8,128)(2,1)}, u32[]{:S(2)}) copy-start(bf16[1,7168,128]{2,1,0:T(8,128)(2,1)} %param.10) | copy-start | bytes 5505028
  3.6 1.2 %copy-start.2 = (bf16[1,1,64,7168]{3,2,1,0:T(8,128)(2,1)S(1)}, bf16[1,1,64,7168]{3,2,1,0:T(8,128)(2,1)}, u32[]{:S(2)}) copy-start(bf16[1,1,64,7168]{3,2,1,0:T(8,128)(2,1)} %param.6) | copy-start | bytes 2752516
  4.8 0.7 copy-start.6
  5.5 0.7 copy-start.7
  79.1 0.6 copy-start.3
  79.8 0.6 copy-start.4
  80.4 0.6 copy-start.5
  81.0 0.6 copy-start.8

commit v2 on v1

v2 whole, which is shorter than its diff:
```python
import functools

import jax
import jax.numpy as jnp
from jax import lax
from jax.experimental import pallas as pl
from jax.experimental.pallas import tpu as pltpu
from jax.sharding import PartitionSpec as P

MESH = pl.DeviceIdType.MESH
BF16 = jnp.bfloat16
F32 = jnp.float32
EXPERTS = 4
N = 8
HALF = N // 2
UNIT = 1024
LANES = 128


def iota(shape, axis):
    return lax.broadcasted_iota(jnp.int32, shape, axis)


def dot(a, b):
    return jnp.dot(a, b, preferred_element_type=F32)


def one_hot(mask):
    return jnp.where(mask, 1.0, 0.0).astype(BF16)


def routing(routes_ref, gates_ref):
    tokens = routes_ref.shape[1]
    rows = EXPERTS * 2 * 8
    row = iota((rows, tokens), 0)
    expert = lax.div(row, 16)
    slot = lax.rem(lax.div(row, 8), 2).astype(F32)
    hits = jnp.zeros((rows, tokens), F32)
    mass = jnp.zeros((rows, tokens), F32)
    for k in range(routes_ref.shape[0]):
        same = routes_ref[k : k + 1, :] == expert
        hits = hits + jnp.where(same, 1.0, 0.0)
        mass = mass + jnp.where(same, gates_ref[k : k + 1, :], 0.0)
    earlier = one_hot(iota((tokens, tokens), 0) < iota((tokens, tokens), 1))
    before = dot(hits.astype(BF16), earlier)
    picks = jnp.where(before == slot, hits, 0.0)
    return picks, mass


def expert_mass(routes_ref, gates_ref):
    tokens = routes_ref.shape[1]
    expert = iota((8, tokens), 0)
    mass = jnp.zeros((8, tokens), F32)
    for k in range(routes_ref.shape[0]):
        same = routes_ref[k : k + 1, :] == expert
        mass = mass + jnp.where(same, gates_ref[k : k + 1, :], 0.0)
    return jnp.broadcast_to(jnp.sum(mass, axis=1, keepdims=True), (8, LANES))


def layer_kernel(
    sizes,
    routes_hbm, gates_hbm, acts_hbm, gate_hbm, up_hbm, down_hbm,
    own_ref, both_ref, pw_ref, mass_z,
    routes_ref, gates_ref,
    acts, w_in, w_out, picked, first_own, first_both, rows, pw_out,
    mass_out, mass_y, mass_x,
    part, rung, send_own, send_both, got_own, got_both, last_own, last_both,
    load_sem, pw_sem, my_sem, mx_sem, mz_sem, fo_sem, fb_sem,
    g_sem, gr_sem, rr_sem, s_sem, lo_sem, lb_sem, keep_sem,
):
    sections, reps, own_units, both_units, pieces = sizes
    own_w, both_w = own_units * UNIT, both_units * UNIT
    tokens = acts.shape[0]
    section, rep, index = (lax.axis_index(a) for a in ("section", "rep", "expert"))
    x, y = lax.rem(index, N), lax.div(index, N)
    expert, side = lax.div(y, 2), lax.rem(y, 2)

    def at(x_, y_):
        return {"expert": lax.rem(y_ + N, N) * N + lax.rem(x_ + N, N)}

    def block(d):
        return lax.rem(x + d + N, N)

    def remote(src, dst, sems, i, device):
        return pltpu.make_async_remote_copy(
            src_ref=src, dst_ref=dst, send_sem=sems.at[(0, *i)], recv_sem=sems.at[(1, *i)],
            device_id=device, device_id_type=MESH,
        )

    sent = []

    def start(copy):
        copy.start()
        sent.append(copy)
        return copy

    def finish():
        for copy in sent:
            copy.wait_send()

    loads = [
        pltpu.make_async_copy(routes_hbm, routes_ref, load_sem.at[0]),
        pltpu.make_async_copy(gates_hbm, gates_ref, load_sem.at[1]),
        pltpu.make_async_copy(acts_hbm, acts, load_sem.at[2]),
        pltpu.make_async_copy(gate_hbm, w_in.at[:, 0:LANES], load_sem.at[3]),
        pltpu.make_async_copy(up_hbm, w_in.at[:, LANES : 2 * LANES], load_sem.at[4]),
        pltpu.make_async_copy(down_hbm, w_out, load_sem.at[5]),
    ]
    for load in loads:
        load.start()

    ahead = {"section": lax.rem(section + 1, sections)}
    behind = {"section": lax.rem(section + sections - 1, sections)}
    barrier = pltpu.get_barrier_semaphore()
    for d in range(1, N):
        for device in (at(x, y + d - N), at(x + d - N, y)):
            pl.semaphore_signal(barrier, inc=1, device_id=device, device_id_type=MESH)
    for d in range(1, reps):

        @pl.when(rep + d < reps)
        def _():
            pl.semaphore_signal(barrier, inc=1, device_id={"rep": rep + d}, device_id_type=MESH)

    for d in range(N):
        pl.semaphore_signal(barrier, inc=1, device_id={**behind, **at(x, y + d - N)}, device_id_type=MESH)

    loads[0].wait()
    loads[1].wait()
    picks, mass = routing(routes_ref, gates_ref)
    pw_out[...] = jnp.where(picks > 0, mass, 0.0).astype(BF16)
    mass_out[0] = expert_mass(routes_ref, gates_ref)
    spread = one_hot(iota((tokens, 8 * tokens), 0) == lax.rem(iota((tokens, 8 * tokens), 1), tokens))
    wide = dot(picks.astype(BF16), spread)
    wide_rows, wide_cols = iota(wide.shape, 0), iota(wide.shape, 1)
    wide = jnp.where(lax.rem(wide_rows, 8) == lax.div(wide_cols, tokens), wide, 0.0).astype(BF16)
    loads[2].wait()

    def pick_unit(u):
        stacked = jnp.concatenate(
            [acts[:, u * UNIT + i * LANES : u * UNIT + (i + 1) * LANES] for i in range(8)], axis=0
        )
        picked[:, u] = dot(wide, stacked).astype(BF16).reshape(EXPERTS, 16, LANES)

    for u in (*range(own_units), *range(own_units + both_units, 2 * own_units + both_units)):
        pick_unit(u)
    pl.semaphore_wait(barrier, (N - 1) * 2 + N + rep)

    own_copies, both_copies, mass_copies = [], [], []
    for d in range(1, N):
        to_y = lax.rem(y + d, N)
        own_copies.append(start(remote(
            picked.at[lax.div(to_y, 2), pl.ds(lax.rem(to_y, 2) * (own_units + both_units), own_units)],
            first_own.at[y], fo_sem, (d,), at(x, to_y),
        )))
    first_own[y] = picked[expert, pl.ds(side * (own_units + both_units), own_units)]
    for u in range(own_units, own_units + both_units):
        pick_unit(u)
    for d in range(1, N):
        to_y = lax.rem(y + d, N)
        both_copies.append(start(remote(
            picked.at[lax.div(to_y, 2), pl.ds(own_units, both_units)],
            first_both.at[y], fb_sem, (d,), at(x, to_y),
        )))
    first_both[y] = picked[expert, pl.ds(own_units, both_units)]
    pw_copy = start(remote(pw_out, pw_ref, pw_sem, (), {**ahead}))
    for d in range(1, N):
        mass_copies.append(start(remote(mass_out.at[0], mass_y.at[y], my_sem, (d,), at(x, y + d - N))))
    mass_y[y] = mass_out[0]

    perm_rows, perm_cols = iota((128, 128), 0), iota((128, 128), 1)

    def inner(k):
        return lax.rem(lax.div(k, 2), 8) * 16 + lax.rem(k, 2) * 8 + lax.div(k, 16)

    gather_perm = one_hot(perm_cols == inner(perm_rows))
    scatter_perm = one_hot(perm_rows == inner(perm_cols))

    def assemble(buf, k):
        mixed = dot(gather_perm, buf[:, k].reshape(128, LANES)).astype(BF16)
        return jnp.concatenate([mixed[i * 16 : (i + 1) * 16] for i in range(8)], axis=1)

    def own_cols(first=0, width=own_w, mine=True):
        which = side if mine else 1 - side
        return pl.ds(pl.multiple_of(which * (own_w + both_w) + first, LANES), width)

    def both_cols(first=0, width=both_w):
        return pl.ds(own_w + first, width)

    def piece_cols(piece, first=0, width=None):
        is_own, start_, width_ = pieces[piece]
        cols = own_cols if is_own else both_cols
        return cols(start_ + first, width or width_)

    own_pieces = [i for i, piece in enumerate(pieces) if piece[0]]

    def gather_copy(piece, way, hop):
        sign = 1 if way == 0 else -1
        width = pieces[piece][2]
        first = 0
        if hop == HALF:
            width //= 2
            first = way * width
        ref = rows.at[block(-sign * (hop - 1)), :, piece_cols(piece, first, width)]
        return remote(ref, ref, g_sem, (piece, way, hop - 1), at(x + sign, y))

    def rung_copy(i, d, piece, first=0, width=None):
        ref = rows.at[block(d), :, piece_cols(piece, first, width)]
        return remote(ref, ref, gr_sem, (i,), at(x, y + 1 - 2 * side))

    gathers = {}
    rungs = []
    for copy in own_copies:
        copy.wait_recv()
    for k in range(own_units):
        rows[x, :, own_cols(k * UNIT, UNIT)] = assemble(first_own, k)
    for piece in own_pieces:
        for way in range(2):
            gathers[piece, way, 1] = start(gather_copy(piece, way, 1))
        rungs.append(start(rung_copy(len(rungs), 0, piece)))
    for copy in both_copies:
        copy.wait_recv()
    for k in range(both_units):
        rows[x, :, both_cols(k * UNIT, UNIT)] = assemble(first_both, k)
    for piece in range(len(pieces)):
        if piece not in own_pieces:
            for way in range(2):
                gathers[piece, way, 1] = start(gather_copy(piece, way, 1))

    def mass_copy(i, d):
        return remote(mass_out.at[2], mass_z.at[rep], mz_sem, (i,), {"rep": rep + d})

    keep = pltpu.make_async_copy(mass_out.at[2], mass_z.at[rep], keep_sem)

    for copy in mass_copies:
        copy.wait_recv()
    mass_out[1] = functools.reduce(jnp.add, [mass_y[i] for i in range(N)])
    mass_x[x] = mass_out[1]
    mass_copies = [
        start(remote(mass_out.at[1], mass_x.at[x], mx_sem, (d,), at(x + d - N, y))) for d in range(1, N)
    ]

    for hop in range(1, HALF):
        for piece in range(len(pieces)):
            for way in range(2):
                gathers[piece, way, hop].wait_recv()
                gathers[piece, way, hop + 1] = start(gather_copy(piece, way, hop + 1))
                if piece in own_pieces:
                    rungs.append(start(rung_copy(len(rungs), (-1 if way == 0 else 1) * hop, piece)))
        if hop == 1:
            for copy in mass_copies:
                copy.wait_recv()
            mass_out[2] = functools.reduce(jnp.add, [mass_x[i] for i in range(N)])
            keep.start()
            for d in range(1, reps):

                @pl.when(rep - d >= 0)
                def _():
                    mass_copy(d, -d).start()

    for piece in own_pieces:
        for way in range(2):
            gathers[piece, way, HALF].wait_recv()
            width = pieces[piece][2] // 2
            rungs.append(start(rung_copy(len(rungs), HALF, piece, way * width, width)))

    step = 512

    def project(total, first, width):
        def body(j, total):
            cols = pl.ds(pl.multiple_of(first + j * step, step), step)
            return total + dot(rows[:, :, cols].reshape(128, step), w_in[cols, :])

        return lax.fori_loop(0, width // step, body, total)

    loads[3].wait()
    loads[4].wait()
    total = project(jnp.zeros((128, 2 * LANES), F32), side * (own_w + both_w), own_w)
    for piece in range(len(pieces)):
        if piece not in own_pieces:
            for way in range(2):
                gathers[piece, way, HALF].wait_recv()
    total = project(total, own_w, both_w)
    for copy in rungs:
        copy.wait_recv()
    total = project(total, (1 - side) * (own_w + both_w), own_w)
    gate, up = total[:, :LANES], total[:, LANES:]
    hidden = (gate / (1.0 + jnp.exp(-gate)) * up).astype(BF16)
    loads[5].wait()

    def down(first, width):
        def body(j, carry):
            cols = pl.ds(pl.multiple_of(first + j * step, step), step)
            part[:, :, cols] = dot(hidden, w_out[:, cols]).astype(BF16).reshape(N, 16, step)
            return carry

        lax.fori_loop(0, width // step, body, 0)

    over = {}

    def hand_over(*blocks):
        for d in blocks:
            over[d] = start(remote(
                part.at[block(d), :, own_cols(mine=False)], rung.at[block(d)],
                rr_sem, (len(over),), at(x, y + 1 - 2 * side),
            ))

    down((1 - side) * (own_w + both_w), own_w)
    hand_over(HALF, HALF - 1, 1 - HALF)

    def scatter_copy(piece, way, hop, src):
        is_own, first, width = pieces[piece]
        if hop == 1:
            width //= 2
        dst = (got_own if is_own else got_both).at[way, hop - 1, :, first : first + width]
        return remote(src, dst, s_sem, (piece, way, hop - 1), at(x + 1 - 2 * way, y))

    scatters = {}
    down(own_w, both_w)
    for piece in range(len(pieces)):
        if piece not in own_pieces:
            half = pieces[piece][2] // 2
            for way in range(2):
                src = part.at[block(HALF), :, piece_cols(piece, way * half, half)]
                scatters[piece, way, 1] = start(scatter_copy(piece, way, 1, src))
    down(side * (own_w + both_w), own_w)

    def mine(piece, d):
        is_own, first, width = pieces[piece]
        value = part[block(d), :, piece_cols(piece)].astype(F32)
        if is_own:
            value = value + rung[block(d), :, first : first + width].astype(F32)
        return value

    over[HALF].wait_recv()
    for piece in own_pieces:
        first, half = pieces[piece][1], pieces[piece][2] // 2
        send_own[0, 0, :, first : first + 2 * half] = mine(piece, HALF).astype(BF16)
        for way in range(2):
            src = send_own.at[0, 0, :, first + way * half : first + (way + 1) * half]
            scatters[piece, way, 1] = start(scatter_copy(piece, way, 1, src))
    hand_over(2, -2)
    for hop in range(2, HALF + 1):
        if hop == 2:
            hand_over(1, -1)
        if hop == 3:
            hand_over(0)
        arrived = set()
        for piece in [i for i in range(len(pieces)) if i not in own_pieces] + own_pieces:
            is_own, first, width = pieces[piece]
            send, got = (send_own, got_own) if is_own else (send_both, got_both)
            for way in range(2):
                d = (1 - 2 * way) * (HALF + 1 - hop)
                if is_own and d not in arrived:
                    over[d].wait_recv()
                    arrived.add(d)
                scatters[piece, way, hop - 1].wait_recv()
                value = mine(piece, d)
                if hop == 2:
                    half = width // 2
                    halves = [value[:, :half], value[:, half:]]
                    halves[way] = halves[way] + got[way, 0, :, first : first + half].astype(F32)
                    value = jnp.concatenate(halves, axis=1)
                else:
                    value = value + got[way, hop - 2, :, first : first + width].astype(F32)
                send[way, hop - 1, :, first : first + width] = value.astype(BF16)
                src = send.at[way, hop - 1, :, first : first + width]
                scatters[piece, way, hop] = start(scatter_copy(piece, way, hop, src))

    last_copies = []
    for is_own in (False, True):
        got, last, landing, sems = (
            (got_own, last_own, own_ref, lo_sem) if is_own else (got_both, last_both, both_ref, lb_sem)
        )
        if is_own:
            over[0].wait_recv()
        values = []
        for piece, (kind, first, width) in enumerate(pieces):
            if kind == is_own:
                value = mine(piece, 0)
                for way in range(2):
                    scatters[piece, way, HALF].wait_recv()
                    value = value + got[way, HALF - 1, :, first : first + width].astype(F32)
                values.append(value.astype(BF16))
        value = jnp.concatenate(values, axis=1)
        for k in range(own_units if is_own else both_units):
            stacked = jnp.concatenate(
                [value[:, k * UNIT + i * LANES : k * UNIT + (i + 1) * LANES] for i in range(8)], axis=0
            )
            last[:, k] = dot(scatter_perm, stacked).astype(BF16).reshape(N, 16, LANES)
        for d in range(N):
            to_y = lax.rem(y + d, N)
            last_copies.append(start(remote(
                last.at[to_y], landing.at[expert, side], sems, (d,), {**ahead, **at(x, to_y)},
            )))

    for d in range(1, reps):

        @pl.when(rep + d < reps)
        def _():
            mass_copy(d, d).wait_recv()
            mass_copy(reps + d, d).start()

    pw_copy.wait_recv()
    for copy in last_copies:
        copy.wait_recv()
    for d in range(1, reps):

        @pl.when(rep - d >= 0)
        def _():
            mass_copy(reps + d, -d).wait_recv()
            mass_copy(d, -d).wait_send()

    for d in range(1, reps):

        @pl.when(rep + d < reps)
        def _():
            mass_copy(reps + d, d).wait_send()

    keep.wait()
    for copy in sent:
        copy.wait_send()


def spread_kernel(
    count, pw_hbm, mass_hbm, both_hbm, own_hbm, handed_hbm, share_ref, pw, mass, both, own, out, in_sem, out_sem
):
    pairs = ((pw_hbm, pw), (mass_hbm, mass), (both_hbm, both), (own_hbm, own))
    loads = [pltpu.make_async_copy(src, dst, in_sem.at[i]) for i, (src, dst) in enumerate(pairs)]
    for load in loads:
        load.start()
    tokens = pw.shape[1]
    own_units, both_units = own.shape[2], both.shape[2]
    copy_row = one_hot(iota((8 * tokens, tokens), 1) == lax.rem(iota((8 * tokens, tokens), 0), tokens))

    def widen(picks):
        wide = lax.dot_general(copy_row, picks, (((1,), (1,)), ((), ())), preferred_element_type=F32)
        wide_rows, wide_cols = iota(wide.shape, 0), iota(wide.shape, 1)
        return jnp.where(lax.rem(wide_cols, 8) == lax.div(wide_rows, tokens), wide, 0.0).astype(BF16)

    loads[0].wait()
    wide_one = widen(pw[...])
    wide_two = widen(jnp.concatenate([pw[e * 16 : e * 16 + 16] for e in range(EXPERTS) for _ in range(2)], axis=0))
    loads[1].wait()
    load = functools.reduce(jnp.add, [mass[i] for i in range(mass.shape[0])])
    lane, row = iota((8, LANES), 1), iota((8, LANES), 0)
    share_ref[...] = jnp.sum(jnp.where(lane == row, load, 0.0), axis=0, keepdims=True)[:, :EXPERTS] / count
    outs = []

    def spread(wide, first, values):
        value = jnp.concatenate(values, axis=1)
        tall = dot(wide, value).astype(BF16)
        for k in range(len(values)):
            for i in range(8):
                column = (first + k) * UNIT + i * LANES
                out[:, column : column + LANES] = tall[i * tokens : (i + 1) * tokens, k * LANES : (k + 1) * LANES]
        cols = pl.ds(first * UNIT, len(values) * UNIT)
        copy = pltpu.make_async_copy(out.at[:, cols], handed_hbm.at[:, cols], out_sem.at[len(outs)])
        copy.start()
        outs.append(copy)

    loads[2].wait()
    spread(wide_two, own_units, [both[:, :, k].reshape(EXPERTS * 32, LANES) for k in range(both_units)])
    loads[3].wait()
    for half in range(2):
        spread(
            wide_one, half * (own_units + both_units),
            [own[:, half, k].reshape(EXPERTS * 16, LANES) for k in range(own_units)],
        )
    for copy in outs:
        copy.wait()


def local(activations, routes, gate_values, w_gate, w_up, w_down):
    acts = activations[0, 0]
    tokens, width = acts.shape
    sections, reps = lax.axis_size("section"), lax.axis_size("rep")
    own_units = width // UNIT * 2 // 7
    both_units = width // UNIT - 2 * own_units
    own_w, both_w = own_units * UNIT, both_units * UNIT
    pieces = (
        (True, 0, own_w // 2), (False, 0, both_w // 2), (True, own_w // 2, own_w // 2), (False, both_w // 2, both_w // 2)
    )
    vmem = pl.BlockSpec(memory_space=pltpu.VMEM)
    hbm = pl.BlockSpec(memory_space=pl.ANY)
    dma = pltpu.SemaphoreType.DMA
    count = float(reps * lax.axis_size("expert") * tokens)
    own_shape = (EXPERTS, 2, own_units, 16, LANES)
    both_shape = (EXPERTS, 2, both_units, 16, LANES)
    pw_shape = (EXPERTS * 16, tokens)
    mass_shape = (reps, 8, LANES)
    own, both, pw, mass = pl.pallas_call(
        functools.partial(layer_kernel, (sections, reps, own_units, both_units, pieces)),
        out_shape=(
            jax.ShapeDtypeStruct(own_shape, BF16),
            jax.ShapeDtypeStruct(both_shape, BF16),
            jax.ShapeDtypeStruct(pw_shape, BF16),
            jax.ShapeDtypeStruct(mass_shape, F32),
        ),
        in_specs=[hbm] * 6,
        out_specs=(hbm,) * 4,
        scratch_shapes=[
            pltpu.VMEM(routes.shape[:1:-1], jnp.int32),
            pltpu.VMEM(routes.shape[:1:-1], F32),
            pltpu.VMEM((tokens, width), BF16),
            pltpu.VMEM((width, 2 * LANES), BF16),
            pltpu.VMEM((LANES, width), BF16),
            pltpu.VMEM((EXPERTS, 2 * own_units + both_units, 16, LANES), BF16),
            pltpu.VMEM((N, own_units, 16, LANES), BF16),
            pltpu.VMEM((N, both_units, 16, LANES), BF16),
            pltpu.VMEM((N, 16, width), BF16),
            pltpu.VMEM((EXPERTS * 16, tokens), BF16),
            pltpu.VMEM((3, 8, LANES), F32),
            pltpu.VMEM((N, 8, LANES), F32),
            pltpu.VMEM((N, 8, LANES), F32),
            pltpu.VMEM((N, 16, width), BF16),
            pltpu.VMEM((N, 16, own_w), BF16),
            pltpu.VMEM((2, HALF, 16, own_w), BF16),
            pltpu.VMEM((2, HALF, 16, both_w), BF16),
            pltpu.VMEM((2, HALF, 16, own_w), BF16),
            pltpu.VMEM((2, HALF, 16, both_w), BF16),
            pltpu.VMEM((N, own_units, 16, LANES), BF16),
            pltpu.VMEM((N, both_units, 16, LANES), BF16),
            dma((6,)),
            dma((2,)),
            dma((2, N)),
            dma((2, N)),
            dma((2, 2 * reps)),
            dma((2, N)),
            dma((2, N)),
            dma((2, len(pieces), 2, HALF)),
            dma((2, (N + 1) * len(pieces))),
            dma((2, N)),
            dma((2, len(pieces), 2, HALF)),
            dma((2, N)),
            dma((2, N)),
            dma,
        ],
        compiler_params=pltpu.CompilerParams(
            collective_id=0, has_side_effects=True, vmem_limit_bytes=60 * 2**20
        ),
        name="layer",
    )(routes[0, 0].T, gate_values[0, 0].T, acts, w_gate[0], w_up[0], w_down[0])
    handed, share = pl.pallas_call(
        functools.partial(spread_kernel, count),
        out_shape=(
            jax.ShapeDtypeStruct((tokens, width), BF16),
            jax.ShapeDtypeStruct((1, EXPERTS), F32),
        ),
        in_specs=[hbm] * 4,
        out_specs=(hbm, vmem),
        scratch_shapes=[
            pltpu.VMEM(pw_shape, BF16),
            pltpu.VMEM(mass_shape, F32),
            pltpu.VMEM(both_shape, BF16),
            pltpu.VMEM(own_shape, BF16),
            pltpu.VMEM((tokens, width), BF16),
            dma((4,)),
            dma((3,)),
        ],
        compiler_params=pltpu.CompilerParams(vmem_limit_bytes=60 * 2**20),
        name="spread",
    )(pw, mass, both, own)
    return handed[None, None], share


def solution(mesh):
    placed = (
        P("section", "rep", "expert", None),
        P("section", "rep", "expert", None),
        P("section", "rep", "expert", None),
        P("section", None, "expert"),
        P("section", None, "expert"),
        P("section", "expert", None),
    )
    return jax.shard_map(
        local,
        mesh=mesh,
        in_specs=placed,
        out_specs=(P("section", "rep", "expert", None), P("section", None)),
        check_vma=False,
    )
```

time: 84.5 us -> 70.7 us (0.84)
  local copies, waits for them, and re-layouts: 7.98 us -> 0 us
  Pallas kernels: 75.6 us -> 69.8 us
    unnamed x18 -> x0, local copies, waits for them, and re-layouts: 7.98 us -> none
    pallas_call x1, Pallas kernels: 72.9 us -> 66.9 us  [local(): pl.pallas_call(functools.partial(layer_kernel, (sections, reps, own_units...]
where the time goes in v2:
time: 70.7 us; the launch traced here: 70.4 us
  Pallas kernels  69.8 us (99%)
    pallas_call x1, Pallas kernels, local(): pl.pallas_call(functools.partial(layer_kernel, (sections, reps, own_units...  66.9 us
    pallas_call x1, Pallas kernels, local(): pl.pallas_call(functools.partial(spread_kernel, count), out_shape=(jax.Sh...  2.88 us

profile of v2, /device:TPU:1, one launch (start us, length us, event | category | flops | bytes accessed | tf_op | source)
XLA Modules:
  0.0 70.4 jit_solution(10047810423743406904)
XLA Ops:
  0.6 66.9 %layer.1 = (bf16[4,2,2,16,128]{4,3,2,1,0:T(8,128)(2,1)}, bf16[4,2,3,16,128]{4,3,2,1,0:T(8,128)(2,1)}, bf16[64,64]{1,0:T(8,128)(2,1)}, f32[4,8,128]{2,1,0:T(8,128)}) custom-call(s32[8,64]{1,0:T(8,128)} %bitcast.15, f32[8,64]{1,0:T(8,128)} %bitcast.16, bf16[64,7168]{1,0:T(8,128)(2,1)} %bitcast.14, bf16[7168,128]{1,0:T(8,128)(2,1)} %bitcast.11, ...), custom_call_target="tpu_custom_call" | custom-call | tf_op jit(solution)/shard_map/layer/pallas_call | solution.py:491
  67.6 2.9 %spread.1 = (bf16[64,7168]{1,0:T(8,128)(2,1)}, f32[1,4]{1,0:T(1,128)}) custom-call(bf16[64,64]{1,0:T(8,128)(2,1)} %get-tuple-element.8.pw_hbm, f32[4,8,128]{2,1,0:T(8,128)} %get-tuple-element.9.mass_hbm, bf16[4,2,3,16,128]{4,3,2,1,0:T(8,128)(2,1)} %get-tuple-element.10.both_hbm, bf16[4,2,2,16,128]{4,3,2,1,0:T(8,128)(2,1)} %get-tuple-element.11.own_hbm), custom_call_target="tpu_custom_call" | custom-call | tf_op jit(solution)/shard_map/spread/pallas_call | solution.py:543

commit v3 on v2

--- a/solution.py
+++ b/solution.py
@@ -87,7 +87,16 @@
             device_id=device, device_id_type=MESH,
         )
 
-    sent = []
+    sent, older = [], []
+
+    def set_aside():
+        older.extend(sent)
+        sent.clear()
+
+    def drain():
+        for copy in older:
+            copy.wait_send()
+        older.clear()
 
     def start(copy):
         copy.start()
@@ -106,7 +115,7 @@
         pltpu.make_async_copy(up_hbm, w_in.at[:, LANES : 2 * LANES], load_sem.at[4]),
         pltpu.make_async_copy(down_hbm, w_out, load_sem.at[5]),
     ]
-    for load in loads:
+    for load in loads[:3]:
         load.start()
 
     ahead = {"section": lax.rem(section + 1, sections)}
@@ -152,6 +161,8 @@
             picked.at[lax.div(to_y, 2), pl.ds(lax.rem(to_y, 2) * (own_units + both_units), own_units)],
             first_own.at[y], fo_sem, (d,), at(x, to_y),
         )))
+    for load in loads[3:]:
+        load.start()
     first_own[y] = picked[expert, pl.ds(side * (own_units + both_units), own_units)]
     for u in range(own_units, own_units + both_units):
         pick_unit(u)
@@ -295,6 +306,8 @@
 
         lax.fori_loop(0, width // step, body, 0)
 
+    set_aside()
+
     over = {}
 
     def hand_over(*blocks):
@@ -339,11 +352,14 @@
             src = send_own.at[0, 0, :, first + way * half : first + (way + 1) * half]
             scatters[piece, way, 1] = start(scatter_copy(piece, way, 1, src))
     hand_over(2, -2)
+    drain()
     for hop in range(2, HALF + 1):
         if hop == 2:
             hand_over(1, -1)
         if hop == 3:
             hand_over(0)
+        if hop == HALF:
+            set_aside()
         arrived = set()
         for piece in [i for i in range(len(pieces)) if i not in own_pieces] + own_pieces:
             is_own, first, width = pieces[piece]
@@ -365,6 +381,8 @@
                 send[way, hop - 1, :, first : first + width] = value.astype(BF16)
                 src = send.at[way, hop - 1, :, first : first + width]
                 scatters[piece, way, hop] = start(scatter_copy(piece, way, hop, src))
+
+    drain()
 
     last_copies = []
     for is_own in (False, True):

time: 70.7 us -> 70.5 us (level)
  no operation moved by 1% of the time
where the time goes in v3:
time: 70.5 us; the launch traced here: 70.3 us
  Pallas kernels  69.6 us (99%)
    pallas_call x1, Pallas kernels, local(): pl.pallas_call(functools.partial(layer_kernel, (sections, reps, own_units...  66.8 us
    pallas_call x1, Pallas kernels, local(): pl.pallas_call(functools.partial(spread_kernel, count), out_shape=(jax.Sh...  2.88 us

profile of v3, /device:TPU:1, one launch (start us, length us, event | category | flops | bytes accessed | tf_op | source)
XLA Modules:
  0.0 70.3 jit_solution(14658945791058416523)
XLA Ops:
  0.6 66.8 %layer.1 = (bf16[4,2,2,16,128]{4,3,2,1,0:T(8,128)(2,1)}, bf16[4,2,3,16,128]{4,3,2,1,0:T(8,128)(2,1)}, bf16[64,64]{1,0:T(8,128)(2,1)}, f32[4,8,128]{2,1,0:T(8,128)}) custom-call(s32[8,64]{1,0:T(8,128)} %bitcast.15, f32[8,64]{1,0:T(8,128)} %bitcast.16, bf16[64,7168]{1,0:T(8,128)(2,1)} %bitcast.14, bf16[7168,128]{1,0:T(8,128)(2,1)} %bitcast.11, ...), custom_call_target="tpu_custom_call" | custom-call | tf_op jit(solution)/shard_map/layer/pallas_call | solution.py:509
  67.4 2.9 %spread.1 = (bf16[64,7168]{1,0:T(8,128)(2,1)}, f32[1,4]{1,0:T(1,128)}) custom-call(bf16[64,64]{1,0:T(8,128)(2,1)} %get-tuple-element.8.pw_hbm, f32[4,8,128]{2,1,0:T(8,128)} %get-tuple-element.9.mass_hbm, bf16[4,2,3,16,128]{4,3,2,1,0:T(8,128)(2,1)} %get-tuple-element.10.both_hbm, bf16[4,2,2,16,128]{4,3,2,1,0:T(8,128)(2,1)} %get-tuple-element.11.own_hbm), custom_call_target="tpu_custom_call" | custom-call | tf_op jit(solution)/shard_map/spread/pallas_call | solution.py:561
